TPU v7x, 512 devices: a whole 4x8x8 slice. The times are simulated.
512 devices in a mesh: row: 4 (over z_lo, core), col: 16 (over x, z_hi), depth: 8 (over y).
Axes of the slice: x: 4, y: 8, z: 8 (z_hi: 4, z_lo: 2; z = z_hi * 2 + z_lo), core: 2. Of those that a mesh axis runs over, the one named last changes fastest.
Arguments:
- matrix: bfloat16 [8192, 8192], P('row', 'col'), may hold values from -6 to 6
- occupancy: int32 [128, 128], P('row', 'col'), may hold values 0 or 1
- filtering: int32 [128, 128], replicated, may hold values 0 or 1
Outputs:
- updated: bfloat16 [8192, 8192], P('row', ('col', 'depth'))
All inputs are finite; a program needn't handle non-finite values. No bound on the sum of `occupancy` on one device may be relied on, other than what follows from the above.
Results may differ from a plain program's by a relative error of at most 0.0095.
Values may be sent and summed in bfloat16 or wider, within the bound.
No kernel may reach another device: no remote copies, remote signals or barrier semaphores. Data moves between devices by JAX's collectives and lax.ppermute only.
A program may use at most 64 MiB of HBM per device.

v0:
```python
import functools

import jax
import jax.numpy as jnp
from jax import lax
from jax.experimental import pallas as pl
from jax.experimental.pallas import tpu as pltpu
from jax.sharding import PartitionSpec as P

BLK = 64
LANES = 128
RING = 4
ALONG_Z = [[x * RING + z for z in range(RING)] for x in range(RING)]
ALONG_X = [[x * RING + z for x in range(RING)] for z in range(RING)]


def stage(first, second, rows=4):
    return [
        [row * RING * RING + place for place in group]
        for row in range(rows)
        for group in (first if row % 2 == 0 else second)
    ]


BF16 = jnp.bfloat16
F32 = jnp.float32
F16 = jnp.float16


def call(kernel, flops=0, moved=1 << 20, vmem=24 << 20, **kwargs):
    return pl.pallas_call(
        kernel,
        compiler_params=pltpu.CompilerParams(vmem_limit_bytes=vmem),
        cost_estimate=pl.CostEstimate(flops=flops, bytes_accessed=moved, transcendentals=0),
        **kwargs,
    )


def spread_tiles(occ_t, cols):
    tiles = occ_t.shape[0]
    tile = lax.broadcasted_iota(jnp.int32, (tiles, cols), 1) // BLK
    spread = (lax.broadcasted_iota(jnp.int32, (tiles, cols), 0) == tile).astype(F32)
    return lax.dot_general(
        occ_t.astype(F32), spread, (((0,), (0,)), ((), ())), preferred_element_type=F32
    )


def left_kernel(where, occ_t, rows, left, table):
    cycles, _, _, cols = rows.shape
    depths = table.shape[0] // cycles
    table[...] = spread_tiles(occ_t[...], cols)
    for a in range(cycles):
        mask = table[pl.ds(a * depths + where[0], 1), :]
        left[a * BLK : (a + 1) * BLK, :] = (rows[a, 0].astype(F32) * mask).astype(BF16)


def left_part(matrix, occupancy, where, depths):
    local_rows, cols = matrix.shape
    cycles = local_rows // (depths * BLK)
    occ_t = occupancy.T
    return call(
        left_kernel,
        vmem=60 << 20,
        out_shape=jax.ShapeDtypeStruct((cycles * BLK, cols), BF16),
        grid_spec=pltpu.PrefetchScalarGridSpec(
            num_scalar_prefetch=1,
            grid=(1,),
            in_specs=[
                pl.BlockSpec(occ_t.shape, lambda i, where: (0, 0)),
                pl.BlockSpec((cycles, 1, BLK, cols), lambda i, where: (0, where[0], 0, 0)),
            ],
            out_specs=pl.BlockSpec((cycles * BLK, cols), lambda i, where: (0, 0)),
            scratch_shapes=[pltpu.VMEM((cycles * depths, cols), F32)],
        ),
    )(where, occ_t, matrix.reshape(cycles, depths, BLK, cols))


def right_kernel(occ_t, rows, right):
    tiles, cols = rows.shape[0] // BLK, rows.shape[1]
    table = spread_tiles(occ_t[...], cols)
    for u in range(tiles):
        part = rows[u * BLK : (u + 1) * BLK, :].astype(F32)
        right[u * BLK : (u + 1) * BLK, :] = (part * table[u : u + 1, :]).astype(BF16)


def right_part(matrix, occupancy):
    return call(
        right_kernel, vmem=30 << 20, out_shape=jax.ShapeDtypeStruct(matrix.shape, BF16)
    )(occupancy.T, matrix)


def filter_kernel(depths, tile_rows, tile_cols, where, filtering, mask):
    rows, cols = mask.shape
    tiles = filtering.shape[0]
    row = lax.broadcasted_iota(jnp.int32, (rows, tiles), 0) // BLK * depths
    of_row = lax.broadcasted_iota(jnp.int32, (rows, tiles), 1) == (
        row + where[1] * tile_rows + where[0]
    )
    col = lax.broadcasted_iota(jnp.int32, (tiles, cols), 1) // BLK + where[2] * tile_cols
    of_col = lax.broadcasted_iota(jnp.int32, (tiles, cols), 0) == col
    spread = jnp.dot(of_row.astype(F32), filtering[...].astype(F32), preferred_element_type=F32)
    mask[...] = jnp.dot(spread, of_col.astype(F32), preferred_element_type=F32).astype(BF16)


def filter_mask(filtering, where, depths, tile_rows, tile_cols):
    shape = (tile_rows // depths * BLK, tile_cols * BLK)
    return call(
        functools.partial(filter_kernel, depths, tile_rows, tile_cols),
        out_shape=jax.ShapeDtypeStruct(shape, BF16),
        grid_spec=pltpu.PrefetchScalarGridSpec(
            num_scalar_prefetch=1,
            grid=(1,),
            in_specs=[pl.BlockSpec(filtering.shape, lambda i, where: (0, 0))],
            out_specs=pl.BlockSpec(shape, lambda i, where: (0, 0)),
        ),
    )(where, filtering)


def step_along_x(row):
    return (row & 1) * 2 + row // 2


def terms_kernel(held, scale, where, right, left, *outs):
    rows, inner = outs[0].shape[-2], left.shape[1]
    total = 0.0
    for a in range(RING):
        lefts = []
        for q in held:
            place = (where[1] + step_along_x(where[1] ^ q)) & (RING - 1)
            place = jnp.where((where[1] & 1) == 0, place * RING + a, a * RING + place)
            at = pl.multiple_of(place * rows, rows)
            lefts.append(left[pl.ds(at, rows), :])
        if len(right.shape) == 2:
            part = right[a * inner : (a + 1) * inner, :]
        else:
            part = [right[y, a * BLK : (a + 1) * BLK, :] for y in range(right.shape[0])]
            part = jnp.concatenate(part, axis=0)
        lefts = jnp.concatenate(lefts, axis=0)
        total = total + jnp.dot(lefts, part, preferred_element_type=F32)
    total = (scale * total).astype(BF16)
    for n in range(len(held)):
        part = total[n * rows : (n + 1) * rows]
        if len(outs) == len(held):
            outs[n][...] = part
        else:
            outs[0][n] = part


def terms_of(right, left, where, scale, rows, held, together=False):
    cols = right.shape[-1]
    vmem = pl.BlockSpec(memory_space=pltpu.VMEM)
    out_shape = [jax.ShapeDtypeStruct((rows, cols), BF16)] * len(held)
    if together:
        out_shape = [jax.ShapeDtypeStruct((len(held), rows, cols), BF16)]
    return call(
        functools.partial(terms_kernel, held, scale),
        flops=2 * rows * len(held) * RING * left.shape[1] * cols,
        moved=2 * (right.size + left.size // 2 + rows * len(held) * cols),
        out_shape=out_shape,
        in_specs=[pl.BlockSpec(memory_space=pltpu.SMEM), vmem, vmem],
        out_specs=[vmem] * len(out_shape),
    )(where, right, left)


def pack_kernel(where, here, near, across, both, out):
    mine = (here[...].astype(F32) + near[...].astype(F32)).astype(BF16).T
    other = (across[...].astype(F32) + both[...].astype(F32)).astype(BF16).T
    first = where[1] < 2
    out[0] = jnp.where(first, mine, other)
    out[1] = jnp.where(first, other, mine)


def pack(parts, where):
    rows, cols = parts[0].shape
    vmem = pl.BlockSpec(memory_space=pltpu.VMEM)
    return call(
        pack_kernel,
        out_shape=jax.ShapeDtypeStruct((2, cols, rows), BF16),
        in_specs=[pl.BlockSpec(memory_space=pltpu.SMEM)] + [vmem] * len(parts),
        out_specs=vmem,
    )(where, *parts)


def own_kernel(where, occ_t, columns, own):
    tiles, _, _ = columns.shape
    turned = jnp.concatenate([columns[t] for t in range(tiles)], axis=0).T
    low = lax.rem(where[0], 2) == 0
    mine = jnp.where(low, turned[:BLK, :].astype(F32), turned[BLK:, :].astype(F32))
    row = lax.broadcasted_iota(jnp.int32, (1, tiles * BLK), 1) // BLK
    mask = jnp.zeros((1, tiles * BLK), F32)
    for t in range(tiles):
        mask = jnp.where(row == t, occ_t[where[0], t].astype(F32), mask)
    own[...] = (mine * mask).astype(BF16)


def own_columns(matrix, occupancy, where):
    local_rows, local_cols = matrix.shape
    tiles = local_rows // BLK
    return call(
        own_kernel,
        out_shape=jax.ShapeDtypeStruct((BLK, local_rows), BF16),
        grid_spec=pltpu.PrefetchScalarGridSpec(
            num_scalar_prefetch=2,
            grid=(1,),
            in_specs=[
                pl.BlockSpec((tiles, BLK, LANES), lambda i, where, occ: (0, 0, where[0] // 2))
            ],
            out_specs=pl.BlockSpec((BLK, local_rows), lambda i, where, occ: (0, 0)),
        ),
    )(where, occupancy.T, matrix.reshape(tiles, BLK, local_cols))


def update_kernel(own, got, out):
    depths, lanes = got.shape[0] // 2, got.shape[2]
    low = lax.broadcasted_iota(jnp.int32, (BLK, LANES), 1) < BLK
    for d in range(0, depths, 2):
        for b in range(lanes // LANES):
            span = slice(b * LANES, (b + 1) * LANES)
            one, two = (
                got[d + s, :, span].astype(F32) + got[depths + d + s, :, span].astype(F32)
                for s in (0, 1)
            )
            even = jnp.where(low, one, pltpu.roll(two, BLK, 1))
            odd = jnp.where(low, pltpu.roll(one, BLK, 1), two)
            for a, cube in ((2 * b, even), (2 * b + 1, odd)):
                at = (a * depths + d) * BLK
                value = 1.5 * own[:, at : at + LANES].astype(F32) - 0.5 * cube
                out[:, at : at + LANES] = value.astype(BF16)


def update(own, got):
    return call(update_kernel, out_shape=jax.ShapeDtypeStruct(own.shape, BF16))(own, got)


def shards(matrix, occupancy, filtering):
    rows = lax.axis_size("row")
    depths = lax.axis_size("depth")
    row, col, depth = (lax.axis_index(name) for name in ("row", "col", "depth"))
    local_rows, local_cols = matrix.shape
    own_rows = local_rows // depths
    scale = (local_rows * rows / 2.0) ** (-0.5)
    where = jnp.stack([depth, row, col]).astype(jnp.int32)

    def gather_col(value, groups):
        return lax.all_gather(
            value, ("row", "col"), axis=0, tiled=True, axis_index_groups=groups
        )

    def swap_row(value, bit):
        return lax.ppermute(value, "row", [(r, r ^ bit) for r in range(rows)])

    def trade_x_and_row(value):
        places = [(r, x, z) for r in range(rows) for x in range(RING) for z in range(RING)]
        route = [
            ((r * RING + x) * RING + z, (x * RING + (x + step_along_x(r)) % RING) * RING + z)
            for r, x, z in places
        ]
        return lax.ppermute(value, ("row", "col"), route)

    def parts_of(right):
        [away] = terms_of(right, left, where, scale, own_rows, (1, 3), together=True)
        near, both = swap_row(away, 1)
        across, here = terms_of(right, left, where, scale, own_rows, (2, 0))
        return here, near, across, both

    def parts_added(right):
        [both] = terms_of(right, left, where, scale, own_rows, (3,))
        both = swap_row(both, 1)
        [across] = terms_of(right, left, where, scale, own_rows, (2,))
        across = (across.astype(F32) + both.astype(F32)).astype(BF16)
        across, later = lax.optimization_barrier((across, where))
        across = swap_row(across, 2)
        near, here = terms_of(right, left, later, scale, own_rows, (1, 0))
        across, here = lax.optimization_barrier((across, here))
        return here, across, swap_row(near, 1)

    def trade_over_chip_and_depth(value):
        groups = [
            [r * depths + d for r in (core, core + 2) for d in range(depths)] for core in range(2)
        ]
        return lax.all_to_all(
            value, ("row", "depth"), 0, 0, tiled=True, axis_index_groups=groups
        )

    piece = left_part(matrix, occupancy, depth.astype(jnp.int32)[None], depths)
    moved = trade_x_and_row(piece.astype(F16))
    right = right_part(matrix, occupancy)
    mask = filter_mask(filtering, where, depths, local_rows // BLK, local_cols // BLK)
    own = own_columns(matrix, occupancy, where)
    right, mask, own, moved = lax.optimization_barrier((right, mask, own, moved))
    left = gather_col(moved, stage(ALONG_Z, ALONG_X))
    left = gather_col(left, stage(ALONG_X, ALONG_Z)).astype(BF16)

    here, across, near = parts_added(right)
    square = sum(part.astype(F32) for part in (here, across, near)) * mask.astype(F32)
    square = square.astype(BF16).astype(F16)
    squares = lax.all_gather(square, "depth", axis=0).astype(BF16)

    parts = pack(parts_of(squares), where).reshape(2 * depths, BLK, own_rows)
    return update(own, trade_over_chip_and_depth(parts)).T


def solution(mesh):
    placed = (P("row", "col"), P("row", "col"), P())
    return jax.shard_map(
        shards, mesh=mesh, in_specs=placed, out_specs=P("row", ("col", "depth")), check_vma=False
    )
```

profile of v0, /device:TPU:6, one launch (start us, length us, event | category | flops | bytes accessed | tf_op | source)
XLA Modules:
  0.0 152.8 jit_solution(12681686508912395940)
XLA Ops:
  0.0 1.9 %shard_map.40 = bf16[256,512]{1,0:T(8,128)(2,1)} custom-call(s32[1]{0:T(128)} %bitcast.1.where, s32[8,32]{1,0:T(8,128)} %bitcast.18, bf16[4,8,64,512]{3,2,1,0:T(8,128)(2,1)} %bitcast.13), custom_call_target="tpu_custom_call" | custom-call | bytes 1048576 | tf_op jit(solution)/shard_map/pallas_call | solution.py:61
  1.9 1.0 convert_element_type.36
  2.9 3.7 %collective-permute-start = (f16[256,512]{1,0:T(8,128)(2,1)S(1)}, f16[256,512]{1,0:T(8,128)(2,1)S(1)}, u32[]{:S(2)}, u32[]{:S(2)}) collective-permute-start(f16[256,512]{1,0:T(8,128)(2,1)S(1)} %convert_element_type.36), channel_id=1, source_target_pairs={{0,0},{8,8},{16,16},{24,24},{32,160},{40,168},{48,176},{56,184},{6... | collective-permute-start | bytes 786440 | tf_op jit(solution)/shard_map/ppermute | solution.py:258
  6.7 1.6 %copy-done = bf16[2048,512]{1,0:T(8,128)(2,1)S(1)} copy-done((bf16[2048,512]{1,0:T(8,128)(2,1)S(1)}, bf16[2048,512]{1,0:T(8,128)(2,1)}, u32[]{:S(2)}) %copy-start) | copy-done | bytes 2097176
  8.9 1.6 %copy-done.1 = bf16[2048,512]{1,0:T(8,128)(2,1)S(1)} copy-done((bf16[2048,512]{1,0:T(8,128)(2,1)S(1)}, bf16[2048,512]{1,0:T(8,128)(2,1)}, u32[]{:S(2)}) %copy-start.1) | copy-done | bytes 2097176
  10.5 0.8 shard_map.39.own
  11.3 0.9 shard_map.38
  12.2 3.2 %collective-permute-done = f16[256,512]{1,0:T(8,128)(2,1)S(1)} collective-permute-done((f16[256,512]{1,0:T(8,128)(2,1)S(1)}, f16[256,512]{1,0:T(8,128)(2,1)S(1)}, u32[]{:S(2)}, u32[]{:S(2)}) %collective-permute-start) | collective-permute-done | bytes 262176 | tf_op jit(solution)/shard_map/ppermute | solution.py:258
  15.4 32.9 %all-gather.4 = f16[1024,512]{1,0:T(8,128)(2,1)S(1)} all-gather(f16[256,512]{1,0:T(8,128)(2,1)S(1)} %collective-permute-done), channel_id=1, replica_groups={{0,8,16,24},{32,40,48,56},{64,72,80,88},{96,104,112,120},{128,160,192,2..., dimensions={0}, use_global_device_ids=true | all-gather | bytes 1310720 | tf_op jit(solution)/shard_map/all_gather | solution.py:245
  48.2 28.3 %all-gather.5 = f16[4096,512]{1,0:T(8,128)(2,1)S(1)} all-gather(f16[1024,512]{1,0:T(8,128)(2,1)S(1)} %all-gather.4), channel_id=1, replica_groups={{0,32,64,96},{8,40,72,104},{16,48,80,112},{24,56,88,120},{128,136,144,1..., dimensions={0}, use_global_device_ids=true | all-gather | bytes 5242880 | tf_op jit(solution)/shard_map/all_gather | solution.py:245
  76.5 0.8 convert_element_type.37.left
  77.4 1.2 shard_map.42
  78.6 1.9 %collective-permute-start.1 = (bf16[256,512]{1,0:T(8,128)(2,1)S(1)}, bf16[256,512]{1,0:T(8,128)(2,1)S(1)}, u32[]{:S(2)}, u32[]{:S(2)}) collective-permute-start(bf16[256,512]{1,0:T(8,128)(2,1)S(1)} %shard_map.42), channel_id=1, source_target_pairs={{0,128},{128,0},{256,384},{384,256},{1,129},{129,1},{257,385},{385... | collective-permute-start | bytes 786440 | tf_op jit(solution)/shard_map/ppermute | solution.py:250
  80.5 1.2 shard_map.41
  82.1 1.9 %collective-permute-start.2 = (bf16[256,512]{1,0:T(8,128)(2,1)S(1)}, bf16[256,512]{1,0:T(8,128)(2,1)S(1)}, u32[]{:S(2)}, u32[]{:S(2)}) collective-permute-start(bf16[256,512]{1,0:T(8,128)(2,1)S(1)} %add_convert_fusion), channel_id=1, source_target_pairs={{0,256},{128,384},{256,0},{384,128},{1,257},{129,385},{257,1},{385... | collective-permute-start | bytes 786440 | tf_op jit(solution)/shard_map/ppermute | solution.py:250
  84.0 1.8 %shard_map.43 = (bf16[256,512]{1,0:T(8,128)(2,1)S(1)}, bf16[256,512]{1,0:T(8,128)(2,1)S(1)}) custom-call(s32[3]{0:T(128)S(1)} %pad_add_fusion.where, bf16[2048,512]{1,0:T(8,128)(2,1)S(1)} %shard_map.37.right, bf16[4096,512]{1,0:T(8,128)(2,1)S(1)} %convert_element_type.37.left), custom_call_target="tpu_custom_call" | custom-call | flops 1073741824 | bytes 4718592 | tf_op jit(solution)/shard_map/pallas_call | solution.py:155
  85.8 2.2 %collective-permute-start.3 = (bf16[256,512]{1,0:T(8,128)(2,1)S(1)}, bf16[256,512]{1,0:T(8,128)(2,1)S(1)}, u32[]{:S(2)}, u32[]{:S(2)}) collective-permute-start(bf16[256,512]{1,0:T(8,128)(2,1)S(1)} %get-tuple-element.25), channel_id=1, source_target_pairs={{0,128},{128,0},{256,384},{384,256},{1,129},{129,1},{257,385},{385... | collective-permute-start | bytes 786440 | tf_op jit(solution)/shard_map/ppermute | solution.py:250
  88.0 4.5 %collective-permute-done.2 = bf16[256,512]{1,0:T(8,128)(2,1)S(1)} collective-permute-done((bf16[256,512]{1,0:T(8,128)(2,1)S(1)}, bf16[256,512]{1,0:T(8,128)(2,1)S(1)}, u32[]{:S(2)}, u32[]{:S(2)}) %collective-permute-start.2) | collective-permute-done | bytes 262176 | tf_op jit(solution)/shard_map/ppermute | solution.py:250
  92.6 31.2 %all-gather.6 = f16[2048,512]{1,0:T(8,128)(2,1)S(1)} all-gather(f16[256,512]{1,0:T(8,128)(2,1)S(1)} %fusion), channel_id=2, replica_groups=mesh['row'=4,'col'=16,'depth'=8] {'depth'}, dimensions={0}, use_global_device_ids=true | all-gather | bytes 2359296 | tf_op jit(solution)/shard_map/all_gather | solution.py:297
  124.3 1.8 %shard_map.45 = bf16[2,256,512]{2,1,0:T(8,128)(2,1)S(1)} custom-call(s32[3]{0:T(128)S(1)} %pad_add_fusion.where, bf16[8,256,512]{2,1,0:T(8,128)(2,1)S(1)} %bitcast.15, bf16[4096,512]{1,0:T(8,128)(2,1)S(1)} %convert_element_type.37.left), custom_call_target="tpu_custom_call" | custom-call | flops 1073741824 | bytes 4718592 | tf_op jit(solution)/shard_map/pallas_call | solution.py:155
  126.1 1.9 %collective-permute-start.4 = (bf16[2,256,512]{2,1,0:T(8,128)(2,1)S(1)}, bf16[2,256,512]{2,1,0:T(8,128)(2,1)S(1)}, u32[]{:S(2)}, u32[]{:S(2)}) collective-permute-start(bf16[2,256,512]{2,1,0:T(8,128)(2,1)S(1)} %shard_map.45), channel_id=1, source_target_pairs={{0,128},{128,0},{256,384},{384,256},{1,129},{129,1},{257,385},{385... | collective-permute-start | bytes 1572872 | tf_op jit(solution)/shard_map/ppermute | solution.py:250
  128.0 1.8 %shard_map.44 = (bf16[256,512]{1,0:T(8,128)(2,1)S(1)}, bf16[256,512]{1,0:T(8,128)(2,1)S(1)}) custom-call(s32[3]{0:T(128)S(1)} %pad_add_fusion.where, bf16[8,256,512]{2,1,0:T(8,128)(2,1)S(1)} %bitcast.16, bf16[4096,512]{1,0:T(8,128)(2,1)S(1)} %convert_element_type.37.left), custom_call_target="tpu_custom_call" | custom-call | flops 1073741824 | bytes 4718592 | tf_op jit(solution)/shard_map/pallas_call | solution.py:155
  130.7 21.2 %all_to_all.5.got = bf16[16,64,256]{2,1,0:T(8,128)(2,1)S(1)} all-to-all(bf16[16,64,256]{2,1,0:T(8,128)(2,1)S(1)} %bitcast.17), channel_id=1, replica_groups={{0,1,2,3,4,5,6,7,256,257,258,259,260,261,262,263},{128,129,130,131,132,..., dimensions={0} | all-to-all | bytes 1048576 | tf_op jit(solution)/shard_map/all_to_all | solution.py:281
  151.9 0.9 shard_map.47
  (16 shorter events, 2.4 us)
Async XLA Ops:
  0.0 6.6 %copy-start.3 = (s32[32,8]{0,1:T(8,128)S(1)}, s32[32,8]{0,1:T(8,128)}, u32[]{:S(2)}) copy-start(s32[32,8]{0,1:T(8,128)} %param.4) | copy-start | bytes 3076
  2.9 12.4 %collective-permute-start = (f16[256,512]{1,0:T(8,128)(2,1)S(1)}, f16[256,512]{1,0:T(8,128)(2,1)S(1)}, u32[]{:S(2)}, u32[]{:S(2)}) collective-permute-start(f16[256,512]{1,0:T(8,128)(2,1)S(1)} %convert_element_type.36), channel_id=1, source_target_pairs={{0,0},{8,8},{16,16},{24,24},{32,160},{40,168},{48,176},{56,184},{6... | collective-permute-start | bytes 786440 | tf_op jit(solution)/shard_map/ppermute | solution.py:258
  6.7 1.6 %copy-start = (bf16[2048,512]{1,0:T(8,128)(2,1)S(1)}, bf16[2048,512]{1,0:T(8,128)(2,1)}, u32[]{:S(2)}) copy-start(bf16[2048,512]{1,0:T(8,128)(2,1)} %rows.1) | copy-start | bytes 6291460
  8.2 3.1 %copy-start.2 = (s32[128,128]{1,0:T(8,128)S(1)}, s32[128,128]{1,0:T(8,128)}, u32[]{:S(2)}) copy-start(s32[128,128]{1,0:T(8,128)} %filtering.1) | copy-start | bytes 196612
  8.9 1.6 %copy-start.1 = (bf16[2048,512]{1,0:T(8,128)(2,1)S(1)}, bf16[2048,512]{1,0:T(8,128)(2,1)}, u32[]{:S(2)}) copy-start(bf16[2048,512]{1,0:T(8,128)(2,1)} %rows.1) | copy-start | bytes 6291460
  78.6 3.4 %collective-permute-start.1 = (bf16[256,512]{1,0:T(8,128)(2,1)S(1)}, bf16[256,512]{1,0:T(8,128)(2,1)S(1)}, u32[]{:S(2)}, u32[]{:S(2)}) collective-permute-start(bf16[256,512]{1,0:T(8,128)(2,1)S(1)} %shard_map.42), channel_id=1, source_target_pairs={{0,128},{128,0},{256,384},{384,256},{1,129},{129,1},{257,385},{385... | collective-permute-start | bytes 786440 | tf_op jit(solution)/shard_map/ppermute | solution.py:250
  82.1 10.4 %collective-permute-start.2 = (bf16[256,512]{1,0:T(8,128)(2,1)S(1)}, bf16[256,512]{1,0:T(8,128)(2,1)S(1)}, u32[]{:S(2)}, u32[]{:S(2)}) collective-permute-start(bf16[256,512]{1,0:T(8,128)(2,1)S(1)} %add_convert_fusion), channel_id=1, source_target_pairs={{0,256},{128,384},{256,0},{384,128},{1,257},{129,385},{257,1},{385... | collective-permute-start | bytes 786440 | tf_op jit(solution)/shard_map/ppermute | solution.py:250
  85.8 6.6 %collective-permute-start.3 = (bf16[256,512]{1,0:T(8,128)(2,1)S(1)}, bf16[256,512]{1,0:T(8,128)(2,1)S(1)}, u32[]{:S(2)}, u32[]{:S(2)}) collective-permute-start(bf16[256,512]{1,0:T(8,128)(2,1)S(1)} %get-tuple-element.25), channel_id=1, source_target_pairs={{0,128},{128,0},{256,384},{384,256},{1,129},{129,1},{257,385},{385... | collective-permute-start | bytes 786440 | tf_op jit(solution)/shard_map/ppermute | solution.py:250
  126.1 3.8 %collective-permute-start.4 = (bf16[2,256,512]{2,1,0:T(8,128)(2,1)S(1)}, bf16[2,256,512]{2,1,0:T(8,128)(2,1)S(1)}, u32[]{:S(2)}, u32[]{:S(2)}) collective-permute-start(bf16[2,256,512]{2,1,0:T(8,128)(2,1)S(1)} %shard_map.45), channel_id=1, source_target_pairs={{0,128},{128,0},{256,384},{384,256},{1,129},{129,1},{257,385},{385... | collective-permute-start | bytes 1572872 | tf_op jit(solution)/shard_map/ppermute | solution.py:250
where the time goes:
time: 156 us; the launch traced here: 153 us
  blocking collectives  114 us (73%)
  Pallas kernels  13.6 us (9%)
  starting transfers between devices  11.6 us (7%)
  waiting for transfers between devices  7.98 us (5%)
  local copies, waits for them, and re-layouts  3.22 us (2%)
  other arithmetic  2.53 us (2%)
    all_gather x2, blocking collectives, gather_col(): lax.all_gather(value, ('row', 'col'), axis=0, tiled=True, axis_index_grou...  61.2 us
    all_gather x1, blocking collectives, shards(): squares = lax.all_gather(square, 'depth', axis=0).astype(BF16)  31.2 us
    all_to_all x1, blocking collectives, trade_over_chip_and_depth(): lax.all_to_all(value, ('row', 'depth'), 0, 0, tiled=True, axis_index_grou...  21.2 us
    ppermute x4, starting transfers between devices, swap_row(): return lax.ppermute(value, 'row', [(r, r ^ bit) for r in range(rows)])  7.93 us
    pallas_call x5, Pallas kernels, terms_of(): call(functools.partial(terms_kernel, held, scale), flops=2 * rows * len(h...  7.84 us
    ppermute x4, waiting for transfers between devices, swap_row(): return lax.ppermute(value, 'row', [(r, r ^ bit) for r in range(rows)])  4.81 us
    ppermute x1, starting transfers between devices, trade_x_and_row(): return lax.ppermute(value, ('row', 'col'), route)  3.72 us
    unnamed x8, local copies, waits for them, and re-layouts  3.19 us
  transfers between devices with their start and end apart: 5, of which 4 were waited for; matrix products, arithmetic and copies ran while one was open for 0% of the time, Pallas kernels for 5%

commit v1 on v0

--- a/solution.py
+++ b/solution.py
@@ -127,7 +127,7 @@
         lefts = []
         for q in held:
             place = (where[1] + step_along_x(where[1] ^ q)) & (RING - 1)
-            place = jnp.where((where[1] & 1) == 0, place * RING + a, a * RING + place)
+            place = jnp.where((where[1] & 1) == 0, a * RING + place, place * RING + a)
             at = pl.multiple_of(place * rows, rows)
             lefts.append(left[pl.ds(at, rows), :])
         if len(right.shape) == 2:
@@ -288,8 +288,8 @@
     mask = filter_mask(filtering, where, depths, local_rows // BLK, local_cols // BLK)
     own = own_columns(matrix, occupancy, where)
     right, mask, own, moved = lax.optimization_barrier((right, mask, own, moved))
-    left = gather_col(moved, stage(ALONG_Z, ALONG_X))
-    left = gather_col(left, stage(ALONG_X, ALONG_Z)).astype(BF16)
+    left = gather_col(moved, stage(ALONG_X, ALONG_Z))
+    left = gather_col(left, stage(ALONG_Z, ALONG_X)).astype(BF16)
 
     here, across, near = parts_added(right)
     square = sum(part.astype(F32) for part in (here, across, near)) * mask.astype(F32)

time: 156 us -> 154 us (0.987)
  the two profiles are of different devices: /device:TPU:6 before, /device:TPU:8 now
where the time goes in v1:
time: 154 us
  blocking collectives  121 us (79%)
  Pallas kernels  13.6 us (9%)
  starting transfers between devices  9.75 us (6%)
  waiting for transfers between devices  3.67 us (2%)
  local copies, waits for them, and re-layouts  3.22 us (2%)
  other arithmetic  2.53 us (2%)
    all_gather x2, blocking collectives, gather_col(): lax.all_gather(value, ('row', 'col'), axis=0, tiled=True, axis_index_grou...  67.2 us
    all_gather x1, blocking collectives, shards(): squares = lax.all_gather(square, 'depth', axis=0).astype(BF16)  30.6 us
    all_to_all x1, blocking collectives, trade_over_chip_and_depth(): lax.all_to_all(value, ('row', 'depth'), 0, 0, tiled=True, axis_index_grou...  23 us
    ppermute x4, starting transfers between devices, swap_row(): return lax.ppermute(value, 'row', [(r, r ^ bit) for r in range(rows)])  9.07 us
    pallas_call x5, Pallas kernels, terms_of(): call(functools.partial(terms_kernel, held, scale), flops=2 * rows * len(h...  7.84 us
    ppermute x4, waiting for transfers between devices, swap_row(): return lax.ppermute(value, 'row', [(r, r ^ bit) for r in range(rows)])  3.67 us
    unnamed x8, local copies, waits for them, and re-layouts  3.19 us
  transfers between devices with their start and end apart: 5, of which 3 were waited for; matrix products, arithmetic and copies ran while one was open for 0% of the time, Pallas kernels for 5%

profile of v1, /device:TPU:8, one launch (start us, length us, event | category | flops | bytes accessed | tf_op | source)
XLA Modules:
  0.0 153.8 jit_solution(4831998173309996557)
XLA Ops:
  0.0 1.9 %shard_map.40 = bf16[256,512]{1,0:T(8,128)(2,1)} custom-call(s32[1]{0:T(128)} %bitcast.1.where, s32[8,32]{1,0:T(8,128)} %bitcast.18, bf16[4,8,64,512]{3,2,1,0:T(8,128)(2,1)} %bitcast.13), custom_call_target="tpu_custom_call" | custom-call | bytes 1048576 | tf_op jit(solution)/shard_map/pallas_call | solution.py:61
  1.9 1.0 convert_element_type.36
  2.9 0.7 collective-permute-start
  3.6 1.6 %copy-done = bf16[2048,512]{1,0:T(8,128)(2,1)S(1)} copy-done((bf16[2048,512]{1,0:T(8,128)(2,1)S(1)}, bf16[2048,512]{1,0:T(8,128)(2,1)}, u32[]{:S(2)}) %copy-start) | copy-done | bytes 2097176
  5.8 1.6 %copy-done.1 = bf16[2048,512]{1,0:T(8,128)(2,1)S(1)} copy-done((bf16[2048,512]{1,0:T(8,128)(2,1)S(1)}, bf16[2048,512]{1,0:T(8,128)(2,1)}, u32[]{:S(2)}) %copy-start.1) | copy-done | bytes 2097176
  7.4 0.8 shard_map.39.own
  8.3 0.9 shard_map.38
  9.1 19.9 %all-gather.4 = f16[1024,512]{1,0:T(8,128)(2,1)S(1)} all-gather(f16[256,512]{1,0:T(8,128)(2,1)S(1)} %collective-permute-done), channel_id=1, replica_groups={{0,32,64,96},{8,40,72,104},{16,48,80,112},{24,56,88,120},{128,136,144,1..., dimensions={0}, use_global_device_ids=true | all-gather | bytes 1310720 | tf_op jit(solution)/shard_map/all_gather | solution.py:245
  29.1 47.3 %all-gather.5 = f16[4096,512]{1,0:T(8,128)(2,1)S(1)} all-gather(f16[1024,512]{1,0:T(8,128)(2,1)S(1)} %all-gather.4), channel_id=1, replica_groups={{0,8,16,24},{32,40,48,56},{64,72,80,88},{96,104,112,120},{128,160,192,2..., dimensions={0}, use_global_device_ids=true | all-gather | bytes 5242880 | tf_op jit(solution)/shard_map/all_gather | solution.py:245
  76.4 0.8 convert_element_type.37.left
  77.2 1.2 shard_map.42
  78.5 1.9 %collective-permute-start.1 = (bf16[256,512]{1,0:T(8,128)(2,1)S(1)}, bf16[256,512]{1,0:T(8,128)(2,1)S(1)}, u32[]{:S(2)}, u32[]{:S(2)}) collective-permute-start(bf16[256,512]{1,0:T(8,128)(2,1)S(1)} %shard_map.42), channel_id=1, source_target_pairs={{0,128},{128,0},{256,384},{384,256},{1,129},{129,1},{257,385},{385... | collective-permute-start | bytes 786440 | tf_op jit(solution)/shard_map/ppermute | solution.py:250
  80.4 1.2 shard_map.41
  82.0 3.3 %collective-permute-start.2 = (bf16[256,512]{1,0:T(8,128)(2,1)S(1)}, bf16[256,512]{1,0:T(8,128)(2,1)S(1)}, u32[]{:S(2)}, u32[]{:S(2)}) collective-permute-start(bf16[256,512]{1,0:T(8,128)(2,1)S(1)} %add_convert_fusion), channel_id=1, source_target_pairs={{0,256},{128,384},{256,0},{384,128},{1,257},{129,385},{257,1},{385... | collective-permute-start | bytes 786440 | tf_op jit(solution)/shard_map/ppermute | solution.py:250
  85.3 1.8 %shard_map.43 = (bf16[256,512]{1,0:T(8,128)(2,1)S(1)}, bf16[256,512]{1,0:T(8,128)(2,1)S(1)}) custom-call(s32[3]{0:T(128)S(1)} %pad_add_fusion.where, bf16[2048,512]{1,0:T(8,128)(2,1)S(1)} %shard_map.37.right, bf16[4096,512]{1,0:T(8,128)(2,1)S(1)} %convert_element_type.37.left), custom_call_target="tpu_custom_call" | custom-call | flops 1073741824 | bytes 4718592 | tf_op jit(solution)/shard_map/pallas_call | solution.py:155
  87.1 1.9 %collective-permute-start.3 = (bf16[256,512]{1,0:T(8,128)(2,1)S(1)}, bf16[256,512]{1,0:T(8,128)(2,1)S(1)}, u32[]{:S(2)}, u32[]{:S(2)}) collective-permute-start(bf16[256,512]{1,0:T(8,128)(2,1)S(1)} %get-tuple-element.25), channel_id=1, source_target_pairs={{0,128},{128,0},{256,384},{384,256},{1,129},{129,1},{257,385},{385... | collective-permute-start | bytes 786440 | tf_op jit(solution)/shard_map/ppermute | solution.py:250
  89.0 3.3 %collective-permute-done.2 = bf16[256,512]{1,0:T(8,128)(2,1)S(1)} collective-permute-done((bf16[256,512]{1,0:T(8,128)(2,1)S(1)}, bf16[256,512]{1,0:T(8,128)(2,1)S(1)}, u32[]{:S(2)}, u32[]{:S(2)}) %collective-permute-start.2) | collective-permute-done | bytes 262176 | tf_op jit(solution)/shard_map/ppermute | solution.py:250
  92.5 30.6 %all-gather.6 = f16[2048,512]{1,0:T(8,128)(2,1)S(1)} all-gather(f16[256,512]{1,0:T(8,128)(2,1)S(1)} %fusion), channel_id=2, replica_groups=mesh['row'=4,'col'=16,'depth'=8] {'depth'}, dimensions={0}, use_global_device_ids=true | all-gather | bytes 2359296 | tf_op jit(solution)/shard_map/all_gather | solution.py:297
  123.5 1.8 %shard_map.45 = bf16[2,256,512]{2,1,0:T(8,128)(2,1)S(1)} custom-call(s32[3]{0:T(128)S(1)} %pad_add_fusion.where, bf16[8,256,512]{2,1,0:T(8,128)(2,1)S(1)} %bitcast.15, bf16[4096,512]{1,0:T(8,128)(2,1)S(1)} %convert_element_type.37.left), custom_call_target="tpu_custom_call" | custom-call | flops 1073741824 | bytes 4718592 | tf_op jit(solution)/shard_map/pallas_call | solution.py:155
  125.3 1.9 %collective-permute-start.4 = (bf16[2,256,512]{2,1,0:T(8,128)(2,1)S(1)}, bf16[2,256,512]{2,1,0:T(8,128)(2,1)S(1)}, u32[]{:S(2)}, u32[]{:S(2)}) collective-permute-start(bf16[2,256,512]{2,1,0:T(8,128)(2,1)S(1)} %shard_map.45), channel_id=1, source_target_pairs={{0,128},{128,0},{256,384},{384,256},{1,129},{129,1},{257,385},{385... | collective-permute-start | bytes 1572872 | tf_op jit(solution)/shard_map/ppermute | solution.py:250
  127.2 1.8 %shard_map.44 = (bf16[256,512]{1,0:T(8,128)(2,1)S(1)}, bf16[256,512]{1,0:T(8,128)(2,1)S(1)}) custom-call(s32[3]{0:T(128)S(1)} %pad_add_fusion.where, bf16[8,256,512]{2,1,0:T(8,128)(2,1)S(1)} %bitcast.16, bf16[4096,512]{1,0:T(8,128)(2,1)S(1)} %convert_element_type.37.left), custom_call_target="tpu_custom_call" | custom-call | flops 1073741824 | bytes 4718592 | tf_op jit(solution)/shard_map/pallas_call | solution.py:155
  129.1 0.7 shard_map.46
  129.9 23.0 %all_to_all.5.got = bf16[16,64,256]{2,1,0:T(8,128)(2,1)S(1)} all-to-all(bf16[16,64,256]{2,1,0:T(8,128)(2,1)S(1)} %bitcast.17), channel_id=1, replica_groups={{0,1,2,3,4,5,6,7,256,257,258,259,260,261,262,263},{128,129,130,131,132,..., dimensions={0} | all-to-all | bytes 1048576 | tf_op jit(solution)/shard_map/all_to_all | solution.py:281
  152.8 0.9 shard_map.47
  (16 shorter events, 1.6 us)
Async XLA Ops:
  0.0 3.6 %copy-start.3 = (s32[32,8]{0,1:T(8,128)S(1)}, s32[32,8]{0,1:T(8,128)}, u32[]{:S(2)}) copy-start(s32[32,8]{0,1:T(8,128)} %param.4) | copy-start | bytes 3076
  2.9 6.2 %collective-permute-start = (f16[256,512]{1,0:T(8,128)(2,1)S(1)}, f16[256,512]{1,0:T(8,128)(2,1)S(1)}, u32[]{:S(2)}, u32[]{:S(2)}) collective-permute-start(f16[256,512]{1,0:T(8,128)(2,1)S(1)} %convert_element_type.36), channel_id=1, source_target_pairs={{0,0},{8,8},{16,16},{24,24},{32,160},{40,168},{48,176},{56,184},{6... | collective-permute-start | bytes 786440 | tf_op jit(solution)/shard_map/ppermute | solution.py:258
  3.6 1.6 %copy-start = (bf16[2048,512]{1,0:T(8,128)(2,1)S(1)}, bf16[2048,512]{1,0:T(8,128)(2,1)}, u32[]{:S(2)}) copy-start(bf16[2048,512]{1,0:T(8,128)(2,1)} %rows.1) | copy-start | bytes 6291460
  5.2 3.1 %copy-start.2 = (s32[128,128]{1,0:T(8,128)S(1)}, s32[128,128]{1,0:T(8,128)}, u32[]{:S(2)}) copy-start(s32[128,128]{1,0:T(8,128)} %filtering.1) | copy-start | bytes 196612
  5.8 1.6 %copy-start.1 = (bf16[2048,512]{1,0:T(8,128)(2,1)S(1)}, bf16[2048,512]{1,0:T(8,128)(2,1)}, u32[]{:S(2)}) copy-start(bf16[2048,512]{1,0:T(8,128)(2,1)} %rows.1) | copy-start | bytes 6291460
  78.5 3.4 %collective-permute-start.1 = (bf16[256,512]{1,0:T(8,128)(2,1)S(1)}, bf16[256,512]{1,0:T(8,128)(2,1)S(1)}, u32[]{:S(2)}, u32[]{:S(2)}) collective-permute-start(bf16[256,512]{1,0:T(8,128)(2,1)S(1)} %shard_map.42), channel_id=1, source_target_pairs={{0,128},{128,0},{256,384},{384,256},{1,129},{129,1},{257,385},{385... | collective-permute-start | bytes 786440 | tf_op jit(solution)/shard_map/ppermute | solution.py:250
  82.0 10.4 %collective-permute-start.2 = (bf16[256,512]{1,0:T(8,128)(2,1)S(1)}, bf16[256,512]{1,0:T(8,128)(2,1)S(1)}, u32[]{:S(2)}, u32[]{:S(2)}) collective-permute-start(bf16[256,512]{1,0:T(8,128)(2,1)S(1)} %add_convert_fusion), channel_id=1, source_target_pairs={{0,256},{128,384},{256,0},{384,128},{1,257},{129,385},{257,1},{385... | collective-permute-start | bytes 786440 | tf_op jit(solution)/shard_map/ppermute | solution.py:250
  87.1 5.3 %collective-permute-start.3 = (bf16[256,512]{1,0:T(8,128)(2,1)S(1)}, bf16[256,512]{1,0:T(8,128)(2,1)S(1)}, u32[]{:S(2)}, u32[]{:S(2)}) collective-permute-start(bf16[256,512]{1,0:T(8,128)(2,1)S(1)} %get-tuple-element.25), channel_id=1, source_target_pairs={{0,128},{128,0},{256,384},{384,256},{1,129},{129,1},{257,385},{385... | collective-permute-start | bytes 786440 | tf_op jit(solution)/shard_map/ppermute | solution.py:250
  125.3 3.8 %collective-permute-start.4 = (bf16[2,256,512]{2,1,0:T(8,128)(2,1)S(1)}, bf16[2,256,512]{2,1,0:T(8,128)(2,1)S(1)}, u32[]{:S(2)}, u32[]{:S(2)}) collective-permute-start(bf16[2,256,512]{2,1,0:T(8,128)(2,1)S(1)} %shard_map.45), channel_id=1, source_target_pairs={{0,128},{128,0},{256,384},{384,256},{1,129},{129,1},{257,385},{385... | collective-permute-start | bytes 1572872 | tf_op jit(solution)/shard_map/ppermute | solution.py:250

commit v2 on v0

--- a/solution.py
+++ b/solution.py
@@ -117,7 +117,7 @@
 
 
 def step_along_x(row):
-    return (row & 1) * 2 + row // 2
+    return (RING - row) & (RING - 1)
 
 
 def terms_kernel(held, scale, where, right, left, *outs):

time: 156 us -> 156 us (level)
  blocking collectives: 114 us -> 116 us
  waiting for transfers between devices: 7.98 us -> 6.01 us
    all_gather x2, blocking collectives: 61.2 us -> 63.4 us  [gather_col(): lax.all_gather(value, ('row', 'col'), axis=0, tiled=True, axis_index_grou...]
    ppermute x1, waiting for transfers between devices: 3.17 us -> 1.2 us  [trade_x_and_row(): return lax.ppermute(value, ('row', 'col'), route)]
where the time goes in v2:
time: 156 us; the launch traced here: 153 us
  blocking collectives  116 us (74%)
  Pallas kernels  13.6 us (9%)
  starting transfers between devices  11.6 us (7%)
  waiting for transfers between devices  6.01 us (4%)
  local copies, waits for them, and re-layouts  3.22 us (2%)
  other arithmetic  2.53 us (2%)
    all_gather x2, blocking collectives, gather_col(): lax.all_gather(value, ('row', 'col'), axis=0, tiled=True, axis_index_grou...  63.4 us
    all_gather x1, blocking collectives, shards(): squares = lax.all_gather(square, 'depth', axis=0).astype(BF16)  31.2 us
    all_to_all x1, blocking collectives, trade_over_chip_and_depth(): lax.all_to_all(value, ('row', 'depth'), 0, 0, tiled=True, axis_index_grou...  21.2 us
    ppermute x4, starting transfers between devices, swap_row(): return lax.ppermute(value, 'row', [(r, r ^ bit) for r in range(rows)])  7.93 us
    pallas_call x5, Pallas kernels, terms_of(): call(functools.partial(terms_kernel, held, scale), flops=2 * rows * len(h...  7.84 us
    ppermute x4, waiting for transfers between devices, swap_row(): return lax.ppermute(value, 'row', [(r, r ^ bit) for r in range(rows)])  4.81 us
    ppermute x1, starting transfers between devices, trade_x_and_row(): return lax.ppermute(value, ('row', 'col'), route)  3.72 us
    unnamed x8, local copies, waits for them, and re-layouts  3.19 us
  transfers between devices with their start and end apart: 5, of which 4 were waited for; matrix products, arithmetic and copies ran while one was open for 0% of the time, Pallas kernels for 5%

profile of v2, /device:TPU:6, one launch (start us, length us, event | category | flops | bytes accessed | tf_op | source)
XLA Modules:
  0.0 153.0 jit_solution(11267392700223195636)
XLA Ops:
  0.0 1.9 %shard_map.40 = bf16[256,512]{1,0:T(8,128)(2,1)} custom-call(s32[1]{0:T(128)} %bitcast.1.where, s32[8,32]{1,0:T(8,128)} %bitcast.18, bf16[4,8,64,512]{3,2,1,0:T(8,128)(2,1)} %bitcast.13), custom_call_target="tpu_custom_call" | custom-call | bytes 1048576 | tf_op jit(solution)/shard_map/pallas_call | solution.py:61
  1.9 1.0 convert_element_type.36
  2.9 3.7 %collective-permute-start = (f16[256,512]{1,0:T(8,128)(2,1)S(1)}, f16[256,512]{1,0:T(8,128)(2,1)S(1)}, u32[]{:S(2)}, u32[]{:S(2)}) collective-permute-start(f16[256,512]{1,0:T(8,128)(2,1)S(1)} %convert_element_type.36), channel_id=1, source_target_pairs={{0,0},{8,8},{16,16},{24,24},{32,160},{40,168},{48,176},{56,184},{6... | collective-permute-start | bytes 786440 | tf_op jit(solution)/shard_map/ppermute | solution.py:258
  6.7 1.6 %copy-done = bf16[2048,512]{1,0:T(8,128)(2,1)S(1)} copy-done((bf16[2048,512]{1,0:T(8,128)(2,1)S(1)}, bf16[2048,512]{1,0:T(8,128)(2,1)}, u32[]{:S(2)}) %copy-start) | copy-done | bytes 2097176
  8.9 1.6 %copy-done.1 = bf16[2048,512]{1,0:T(8,128)(2,1)S(1)} copy-done((bf16[2048,512]{1,0:T(8,128)(2,1)S(1)}, bf16[2048,512]{1,0:T(8,128)(2,1)}, u32[]{:S(2)}) %copy-start.1) | copy-done | bytes 2097176
  10.5 0.8 shard_map.39.own
  11.3 0.9 shard_map.38
  12.2 1.2 collective-permute-done
  13.4 27.4 %all-gather.4 = f16[1024,512]{1,0:T(8,128)(2,1)S(1)} all-gather(f16[256,512]{1,0:T(8,128)(2,1)S(1)} %collective-permute-done), channel_id=1, replica_groups={{0,8,16,24},{32,40,48,56},{64,72,80,88},{96,104,112,120},{128,160,192,2..., dimensions={0}, use_global_device_ids=true | all-gather | bytes 1310720 | tf_op jit(solution)/shard_map/all_gather | solution.py:245
  40.8 36.0 %all-gather.5 = f16[4096,512]{1,0:T(8,128)(2,1)S(1)} all-gather(f16[1024,512]{1,0:T(8,128)(2,1)S(1)} %all-gather.4), channel_id=1, replica_groups={{0,32,64,96},{8,40,72,104},{16,48,80,112},{24,56,88,120},{128,136,144,1..., dimensions={0}, use_global_device_ids=true | all-gather | bytes 5242880 | tf_op jit(solution)/shard_map/all_gather | solution.py:245
  76.8 0.8 convert_element_type.37.left
  77.6 1.2 shard_map.42
  78.9 1.9 %collective-permute-start.1 = (bf16[256,512]{1,0:T(8,128)(2,1)S(1)}, bf16[256,512]{1,0:T(8,128)(2,1)S(1)}, u32[]{:S(2)}, u32[]{:S(2)}) collective-permute-start(bf16[256,512]{1,0:T(8,128)(2,1)S(1)} %shard_map.42), channel_id=1, source_target_pairs={{0,128},{128,0},{256,384},{384,256},{1,129},{129,1},{257,385},{385... | collective-permute-start | bytes 786440 | tf_op jit(solution)/shard_map/ppermute | solution.py:250
  80.8 1.2 shard_map.41
  82.4 1.9 %collective-permute-start.2 = (bf16[256,512]{1,0:T(8,128)(2,1)S(1)}, bf16[256,512]{1,0:T(8,128)(2,1)S(1)}, u32[]{:S(2)}, u32[]{:S(2)}) collective-permute-start(bf16[256,512]{1,0:T(8,128)(2,1)S(1)} %add_convert_fusion), channel_id=1, source_target_pairs={{0,256},{128,384},{256,0},{384,128},{1,257},{129,385},{257,1},{385... | collective-permute-start | bytes 786440 | tf_op jit(solution)/shard_map/ppermute | solution.py:250
  84.3 1.8 %shard_map.43 = (bf16[256,512]{1,0:T(8,128)(2,1)S(1)}, bf16[256,512]{1,0:T(8,128)(2,1)S(1)}) custom-call(s32[3]{0:T(128)S(1)} %pad_add_fusion.where, bf16[2048,512]{1,0:T(8,128)(2,1)S(1)} %shard_map.37.right, bf16[4096,512]{1,0:T(8,128)(2,1)S(1)} %convert_element_type.37.left), custom_call_target="tpu_custom_call" | custom-call | flops 1073741824 | bytes 4718592 | tf_op jit(solution)/shard_map/pallas_call | solution.py:155
  86.1 2.2 %collective-permute-start.3 = (bf16[256,512]{1,0:T(8,128)(2,1)S(1)}, bf16[256,512]{1,0:T(8,128)(2,1)S(1)}, u32[]{:S(2)}, u32[]{:S(2)}) collective-permute-start(bf16[256,512]{1,0:T(8,128)(2,1)S(1)} %get-tuple-element.25), channel_id=1, source_target_pairs={{0,128},{128,0},{256,384},{384,256},{1,129},{129,1},{257,385},{385... | collective-permute-start | bytes 786440 | tf_op jit(solution)/shard_map/ppermute | solution.py:250
  88.3 4.5 %collective-permute-done.2 = bf16[256,512]{1,0:T(8,128)(2,1)S(1)} collective-permute-done((bf16[256,512]{1,0:T(8,128)(2,1)S(1)}, bf16[256,512]{1,0:T(8,128)(2,1)S(1)}, u32[]{:S(2)}, u32[]{:S(2)}) %collective-permute-start.2) | collective-permute-done | bytes 262176 | tf_op jit(solution)/shard_map/ppermute | solution.py:250
  92.9 31.2 %all-gather.6 = f16[2048,512]{1,0:T(8,128)(2,1)S(1)} all-gather(f16[256,512]{1,0:T(8,128)(2,1)S(1)} %fusion), channel_id=2, replica_groups=mesh['row'=4,'col'=16,'depth'=8] {'depth'}, dimensions={0}, use_global_device_ids=true | all-gather | bytes 2359296 | tf_op jit(solution)/shard_map/all_gather | solution.py:297
  124.5 1.8 %shard_map.45 = bf16[2,256,512]{2,1,0:T(8,128)(2,1)S(1)} custom-call(s32[3]{0:T(128)S(1)} %pad_add_fusion.where, bf16[8,256,512]{2,1,0:T(8,128)(2,1)S(1)} %bitcast.15, bf16[4096,512]{1,0:T(8,128)(2,1)S(1)} %convert_element_type.37.left), custom_call_target="tpu_custom_call" | custom-call | flops 1073741824 | bytes 4718592 | tf_op jit(solution)/shard_map/pallas_call | solution.py:155
  126.3 1.9 %collective-permute-start.4 = (bf16[2,256,512]{2,1,0:T(8,128)(2,1)S(1)}, bf16[2,256,512]{2,1,0:T(8,128)(2,1)S(1)}, u32[]{:S(2)}, u32[]{:S(2)}) collective-permute-start(bf16[2,256,512]{2,1,0:T(8,128)(2,1)S(1)} %shard_map.45), channel_id=1, source_target_pairs={{0,128},{128,0},{256,384},{384,256},{1,129},{129,1},{257,385},{385... | collective-permute-start | bytes 1572872 | tf_op jit(solution)/shard_map/ppermute | solution.py:250
  128.3 1.8 %shard_map.44 = (bf16[256,512]{1,0:T(8,128)(2,1)S(1)}, bf16[256,512]{1,0:T(8,128)(2,1)S(1)}) custom-call(s32[3]{0:T(128)S(1)} %pad_add_fusion.where, bf16[8,256,512]{2,1,0:T(8,128)(2,1)S(1)} %bitcast.16, bf16[4096,512]{1,0:T(8,128)(2,1)S(1)} %convert_element_type.37.left), custom_call_target="tpu_custom_call" | custom-call | flops 1073741824 | bytes 4718592 | tf_op jit(solution)/shard_map/pallas_call | solution.py:155
  130.9 21.2 %all_to_all.5.got = bf16[16,64,256]{2,1,0:T(8,128)(2,1)S(1)} all-to-all(bf16[16,64,256]{2,1,0:T(8,128)(2,1)S(1)} %bitcast.17), channel_id=1, replica_groups={{0,1,2,3,4,5,6,7,256,257,258,259,260,261,262,263},{128,129,130,131,132,..., dimensions={0} | all-to-all | bytes 1048576 | tf_op jit(solution)/shard_map/all_to_all | solution.py:281
  152.1 0.9 shard_map.47
  (16 shorter events, 2.4 us)
Async XLA Ops:
  0.0 6.6 %copy-start.3 = (s32[32,8]{0,1:T(8,128)S(1)}, s32[32,8]{0,1:T(8,128)}, u32[]{:S(2)}) copy-start(s32[32,8]{0,1:T(8,128)} %param.4) | copy-start | bytes 3076
  2.9 10.5 %collective-permute-start = (f16[256,512]{1,0:T(8,128)(2,1)S(1)}, f16[256,512]{1,0:T(8,128)(2,1)S(1)}, u32[]{:S(2)}, u32[]{:S(2)}) collective-permute-start(f16[256,512]{1,0:T(8,128)(2,1)S(1)} %convert_element_type.36), channel_id=1, source_target_pairs={{0,0},{8,8},{16,16},{24,24},{32,160},{40,168},{48,176},{56,184},{6... | collective-permute-start | bytes 786440 | tf_op jit(solution)/shard_map/ppermute | solution.py:258
  6.7 1.6 %copy-start = (bf16[2048,512]{1,0:T(8,128)(2,1)S(1)}, bf16[2048,512]{1,0:T(8,128)(2,1)}, u32[]{:S(2)}) copy-start(bf16[2048,512]{1,0:T(8,128)(2,1)} %rows.1) | copy-start | bytes 6291460
  8.2 3.1 %copy-start.2 = (s32[128,128]{1,0:T(8,128)S(1)}, s32[128,128]{1,0:T(8,128)}, u32[]{:S(2)}) copy-start(s32[128,128]{1,0:T(8,128)} %filtering.1) | copy-start | bytes 196612
  8.9 1.6 %copy-start.1 = (bf16[2048,512]{1,0:T(8,128)(2,1)S(1)}, bf16[2048,512]{1,0:T(8,128)(2,1)}, u32[]{:S(2)}) copy-start(bf16[2048,512]{1,0:T(8,128)(2,1)} %rows.1) | copy-start | bytes 6291460
  78.9 3.4 %collective-permute-start.1 = (bf16[256,512]{1,0:T(8,128)(2,1)S(1)}, bf16[256,512]{1,0:T(8,128)(2,1)S(1)}, u32[]{:S(2)}, u32[]{:S(2)}) collective-permute-start(bf16[256,512]{1,0:T(8,128)(2,1)S(1)} %shard_map.42), channel_id=1, source_target_pairs={{0,128},{128,0},{256,384},{384,256},{1,129},{129,1},{257,385},{385... | collective-permute-start | bytes 786440 | tf_op jit(solution)/shard_map/ppermute | solution.py:250
  82.4 10.4 %collective-permute-start.2 = (bf16[256,512]{1,0:T(8,128)(2,1)S(1)}, bf16[256,512]{1,0:T(8,128)(2,1)S(1)}, u32[]{:S(2)}, u32[]{:S(2)}) collective-permute-start(bf16[256,512]{1,0:T(8,128)(2,1)S(1)} %add_convert_fusion), channel_id=1, source_target_pairs={{0,256},{128,384},{256,0},{384,128},{1,257},{129,385},{257,1},{385... | collective-permute-start | bytes 786440 | tf_op jit(solution)/shard_map/ppermute | solution.py:250
  86.1 6.6 %collective-permute-start.3 = (bf16[256,512]{1,0:T(8,128)(2,1)S(1)}, bf16[256,512]{1,0:T(8,128)(2,1)S(1)}, u32[]{:S(2)}, u32[]{:S(2)}) collective-permute-start(bf16[256,512]{1,0:T(8,128)(2,1)S(1)} %get-tuple-element.25), channel_id=1, source_target_pairs={{0,128},{128,0},{256,384},{384,256},{1,129},{129,1},{257,385},{385... | collective-permute-start | bytes 786440 | tf_op jit(solution)/shard_map/ppermute | solution.py:250
  126.3 3.8 %collective-permute-start.4 = (bf16[2,256,512]{2,1,0:T(8,128)(2,1)S(1)}, bf16[2,256,512]{2,1,0:T(8,128)(2,1)S(1)}, u32[]{:S(2)}, u32[]{:S(2)}) collective-permute-start(bf16[2,256,512]{2,1,0:T(8,128)(2,1)S(1)} %shard_map.45), channel_id=1, source_target_pairs={{0,128},{128,0},{256,384},{384,256},{1,129},{129,1},{257,385},{385... | collective-permute-start | bytes 1572872 | tf_op jit(solution)/shard_map/ppermute | solution.py:250

commit v3 on v1

--- a/solution.py
+++ b/solution.py
@@ -133,7 +133,10 @@
         if len(right.shape) == 2:
             part = right[a * inner : (a + 1) * inner, :]
         else:
-            part = [right[y, a * BLK : (a + 1) * BLK, :] for y in range(right.shape[0])]
+            last = (right.shape[0] - 1) * (where[1] & 1)
+            part = [
+                right[jnp.abs(y - last), a * BLK : (a + 1) * BLK, :] for y in range(right.shape[0])
+            ]
             part = jnp.concatenate(part, axis=0)
         lefts = jnp.concatenate(lefts, axis=0)
         total = total + jnp.dot(lefts, part, preferred_element_type=F32)
@@ -294,7 +297,12 @@
     here, across, near = parts_added(right)
     square = sum(part.astype(F32) for part in (here, across, near)) * mask.astype(F32)
     square = square.astype(BF16).astype(F16)
-    squares = lax.all_gather(square, "depth", axis=0).astype(BF16)
+    groups = [
+        [r * depths + (d if r % 2 == 0 else depths - 1 - d) for d in range(depths)]
+        for r in range(rows)
+    ]
+    squares = lax.all_gather(square, ("row", "depth"), axis=0, axis_index_groups=groups)
+    squares = squares.astype(BF16)
 
     parts = pack(parts_of(squares), where).reshape(2 * depths, BLK, own_rows)
     return update(own, trade_over_chip_and_depth(parts)).T

time: 154 us -> 154 us (level)
  no operation moved by 1% of the time
where the time goes in v3:
time: 154 us
  blocking collectives  121 us (79%)
  Pallas kernels  13.7 us (9%)
  starting transfers between devices  9.75 us (6%)
  waiting for transfers between devices  3.66 us (2%)
  local copies, waits for them, and re-layouts  3.22 us (2%)
  other arithmetic  2.53 us (2%)
    all_gather x2, blocking collectives, gather_col(): lax.all_gather(value, ('row', 'col'), axis=0, tiled=True, axis_index_grou...  67.2 us
    all_gather x1, blocking collectives, shards(): lax.all_gather(square, ('row', 'depth'), axis=0, axis_index_groups=groups)  30.6 us
    all_to_all x1, blocking collectives, trade_over_chip_and_depth(): lax.all_to_all(value, ('row', 'depth'), 0, 0, tiled=True, axis_index_grou...  23 us
    ppermute x4, starting transfers between devices, swap_row(): return lax.ppermute(value, 'row', [(r, r ^ bit) for r in range(rows)])  9.07 us
    pallas_call x5, Pallas kernels, terms_of(): call(functools.partial(terms_kernel, held, scale), flops=2 * rows * len(h...  7.86 us
    ppermute x4, waiting for transfers between devices, swap_row(): return lax.ppermute(value, 'row', [(r, r ^ bit) for r in range(rows)])  3.66 us
    unnamed x8, local copies, waits for them, and re-layouts  3.19 us
  transfers between devices with their start and end apart: 5, of which 3 were waited for; matrix products, arithmetic and copies ran while one was open for 0% of the time, Pallas kernels for 5%

profile of v3, /device:TPU:8, one launch (start us, length us, event | category | flops | bytes accessed | tf_op | source)
XLA Modules:
  0.0 153.8 jit_solution(18412011118082595174)
XLA Ops:
  0.0 1.9 %shard_map.40 = bf16[256,512]{1,0:T(8,128)(2,1)} custom-call(s32[1]{0:T(128)} %bitcast.1.where, s32[8,32]{1,0:T(8,128)} %bitcast.18, bf16[4,8,64,512]{3,2,1,0:T(8,128)(2,1)} %bitcast.13), custom_call_target="tpu_custom_call" | custom-call | bytes 1048576 | tf_op jit(solution)/shard_map/pallas_call | solution.py:61
  1.9 1.0 convert_element_type.36
  2.9 0.7 collective-permute-start
  3.6 1.6 %copy-done = bf16[2048,512]{1,0:T(8,128)(2,1)S(1)} copy-done((bf16[2048,512]{1,0:T(8,128)(2,1)S(1)}, bf16[2048,512]{1,0:T(8,128)(2,1)}, u32[]{:S(2)}) %copy-start) | copy-done | bytes 2097176
  5.8 1.6 %copy-done.1 = bf16[2048,512]{1,0:T(8,128)(2,1)S(1)} copy-done((bf16[2048,512]{1,0:T(8,128)(2,1)S(1)}, bf16[2048,512]{1,0:T(8,128)(2,1)}, u32[]{:S(2)}) %copy-start.1) | copy-done | bytes 2097176
  7.4 0.8 shard_map.39.own
  8.3 0.9 shard_map.38
  9.1 19.9 %all-gather.4 = f16[1024,512]{1,0:T(8,128)(2,1)S(1)} all-gather(f16[256,512]{1,0:T(8,128)(2,1)S(1)} %collective-permute-done), channel_id=1, replica_groups={{0,32,64,96},{8,40,72,104},{16,48,80,112},{24,56,88,120},{128,136,144,1..., dimensions={0}, use_global_device_ids=true | all-gather | bytes 1310720 | tf_op jit(solution)/shard_map/all_gather | solution.py:248
  29.1 47.3 %all-gather.5 = f16[4096,512]{1,0:T(8,128)(2,1)S(1)} all-gather(f16[1024,512]{1,0:T(8,128)(2,1)S(1)} %all-gather.4), channel_id=1, replica_groups={{0,8,16,24},{32,40,48,56},{64,72,80,88},{96,104,112,120},{128,160,192,2..., dimensions={0}, use_global_device_ids=true | all-gather | bytes 5242880 | tf_op jit(solution)/shard_map/all_gather | solution.py:248
  76.4 0.8 convert_element_type.37.left
  77.2 1.2 shard_map.42
  78.5 1.9 %collective-permute-start.1 = (bf16[256,512]{1,0:T(8,128)(2,1)S(1)}, bf16[256,512]{1,0:T(8,128)(2,1)S(1)}, u32[]{:S(2)}, u32[]{:S(2)}) collective-permute-start(bf16[256,512]{1,0:T(8,128)(2,1)S(1)} %shard_map.42), channel_id=1, source_target_pairs={{0,128},{128,0},{256,384},{384,256},{1,129},{129,1},{257,385},{385... | collective-permute-start | bytes 786440 | tf_op jit(solution)/shard_map/ppermute | solution.py:253
  80.4 1.2 shard_map.41
  82.0 3.3 %collective-permute-start.2 = (bf16[256,512]{1,0:T(8,128)(2,1)S(1)}, bf16[256,512]{1,0:T(8,128)(2,1)S(1)}, u32[]{:S(2)}, u32[]{:S(2)}) collective-permute-start(bf16[256,512]{1,0:T(8,128)(2,1)S(1)} %add_convert_fusion), channel_id=1, source_target_pairs={{0,256},{128,384},{256,0},{384,128},{1,257},{129,385},{257,1},{385... | collective-permute-start | bytes 786440 | tf_op jit(solution)/shard_map/ppermute | solution.py:253
  85.3 1.8 %shard_map.43 = (bf16[256,512]{1,0:T(8,128)(2,1)S(1)}, bf16[256,512]{1,0:T(8,128)(2,1)S(1)}) custom-call(s32[3]{0:T(128)S(1)} %pad_add_fusion.where, bf16[2048,512]{1,0:T(8,128)(2,1)S(1)} %shard_map.37.right, bf16[4096,512]{1,0:T(8,128)(2,1)S(1)} %convert_element_type.37.left), custom_call_target="tpu_custom_call" | custom-call | flops 1073741824 | bytes 4718592 | tf_op jit(solution)/shard_map/pallas_call | solution.py:158
  87.1 1.9 %collective-permute-start.3 = (bf16[256,512]{1,0:T(8,128)(2,1)S(1)}, bf16[256,512]{1,0:T(8,128)(2,1)S(1)}, u32[]{:S(2)}, u32[]{:S(2)}) collective-permute-start(bf16[256,512]{1,0:T(8,128)(2,1)S(1)} %get-tuple-element.25), channel_id=1, source_target_pairs={{0,128},{128,0},{256,384},{384,256},{1,129},{129,1},{257,385},{385... | collective-permute-start | bytes 786440 | tf_op jit(solution)/shard_map/ppermute | solution.py:253
  89.0 3.3 %collective-permute-done.2 = bf16[256,512]{1,0:T(8,128)(2,1)S(1)} collective-permute-done((bf16[256,512]{1,0:T(8,128)(2,1)S(1)}, bf16[256,512]{1,0:T(8,128)(2,1)S(1)}, u32[]{:S(2)}, u32[]{:S(2)}) %collective-permute-start.2) | collective-permute-done | bytes 262176 | tf_op jit(solution)/shard_map/ppermute | solution.py:253
  92.5 30.6 %all-gather.6 = f16[2048,512]{1,0:T(8,128)(2,1)S(1)} all-gather(f16[256,512]{1,0:T(8,128)(2,1)S(1)} %fusion), channel_id=2, replica_groups={{0,1,2,3,4,5,6,7},{135,134,133,132,131,130,129,128},{256,257,258,259,26..., dimensions={0}, use_global_device_ids=true | all-gather | bytes 2359296 | tf_op jit(solution)/shard_map/all_gather | solution.py:304
  123.5 1.8 %shard_map.45 = bf16[2,256,512]{2,1,0:T(8,128)(2,1)S(1)} custom-call(s32[3]{0:T(128)S(1)} %pad_add_fusion.where, bf16[8,256,512]{2,1,0:T(8,128)(2,1)S(1)} %bitcast.15, bf16[4096,512]{1,0:T(8,128)(2,1)S(1)} %convert_element_type.37.left), custom_call_target="tpu_custom_call" | custom-call | flops 1073741824 | bytes 4718592 | tf_op jit(solution)/shard_map/pallas_call | solution.py:158
  125.3 1.9 %collective-permute-start.4 = (bf16[2,256,512]{2,1,0:T(8,128)(2,1)S(1)}, bf16[2,256,512]{2,1,0:T(8,128)(2,1)S(1)}, u32[]{:S(2)}, u32[]{:S(2)}) collective-permute-start(bf16[2,256,512]{2,1,0:T(8,128)(2,1)S(1)} %shard_map.45), channel_id=1, source_target_pairs={{0,128},{128,0},{256,384},{384,256},{1,129},{129,1},{257,385},{385... | collective-permute-start | bytes 1572872 | tf_op jit(solution)/shard_map/ppermute | solution.py:253
  127.2 1.8 %shard_map.44 = (bf16[256,512]{1,0:T(8,128)(2,1)S(1)}, bf16[256,512]{1,0:T(8,128)(2,1)S(1)}) custom-call(s32[3]{0:T(128)S(1)} %pad_add_fusion.where, bf16[8,256,512]{2,1,0:T(8,128)(2,1)S(1)} %bitcast.16, bf16[4096,512]{1,0:T(8,128)(2,1)S(1)} %convert_element_type.37.left), custom_call_target="tpu_custom_call" | custom-call | flops 1073741824 | bytes 4718592 | tf_op jit(solution)/shard_map/pallas_call | solution.py:158
  129.1 0.7 shard_map.46
  129.9 23.0 %all_to_all.5.got = bf16[16,64,256]{2,1,0:T(8,128)(2,1)S(1)} all-to-all(bf16[16,64,256]{2,1,0:T(8,128)(2,1)S(1)} %bitcast.17), channel_id=1, replica_groups={{0,1,2,3,4,5,6,7,256,257,258,259,260,261,262,263},{128,129,130,131,132,..., dimensions={0} | all-to-all | bytes 1048576 | tf_op jit(solution)/shard_map/all_to_all | solution.py:284
  152.8 0.9 shard_map.47
  (16 shorter events, 1.6 us)
Async XLA Ops:
  0.0 3.6 %copy-start.3 = (s32[32,8]{0,1:T(8,128)S(1)}, s32[32,8]{0,1:T(8,128)}, u32[]{:S(2)}) copy-start(s32[32,8]{0,1:T(8,128)} %param.4) | copy-start | bytes 3076
  2.9 6.2 %collective-permute-start = (f16[256,512]{1,0:T(8,128)(2,1)S(1)}, f16[256,512]{1,0:T(8,128)(2,1)S(1)}, u32[]{:S(2)}, u32[]{:S(2)}) collective-permute-start(f16[256,512]{1,0:T(8,128)(2,1)S(1)} %convert_element_type.36), channel_id=1, source_target_pairs={{0,0},{8,8},{16,16},{24,24},{32,160},{40,168},{48,176},{56,184},{6... | collective-permute-start | bytes 786440 | tf_op jit(solution)/shard_map/ppermute | solution.py:261
  3.6 1.6 %copy-start = (bf16[2048,512]{1,0:T(8,128)(2,1)S(1)}, bf16[2048,512]{1,0:T(8,128)(2,1)}, u32[]{:S(2)}) copy-start(bf16[2048,512]{1,0:T(8,128)(2,1)} %rows.1) | copy-start | bytes 6291460
  5.2 3.1 %copy-start.2 = (s32[128,128]{1,0:T(8,128)S(1)}, s32[128,128]{1,0:T(8,128)}, u32[]{:S(2)}) copy-start(s32[128,128]{1,0:T(8,128)} %filtering.1) | copy-start | bytes 196612
  5.8 1.6 %copy-start.1 = (bf16[2048,512]{1,0:T(8,128)(2,1)S(1)}, bf16[2048,512]{1,0:T(8,128)(2,1)}, u32[]{:S(2)}) copy-start(bf16[2048,512]{1,0:T(8,128)(2,1)} %rows.1) | copy-start | bytes 6291460
  78.5 3.4 %collective-permute-start.1 = (bf16[256,512]{1,0:T(8,128)(2,1)S(1)}, bf16[256,512]{1,0:T(8,128)(2,1)S(1)}, u32[]{:S(2)}, u32[]{:S(2)}) collective-permute-start(bf16[256,512]{1,0:T(8,128)(2,1)S(1)} %shard_map.42), channel_id=1, source_target_pairs={{0,128},{128,0},{256,384},{384,256},{1,129},{129,1},{257,385},{385... | collective-permute-start | bytes 786440 | tf_op jit(solution)/shard_map/ppermute | solution.py:253
  82.0 10.4 %collective-permute-start.2 = (bf16[256,512]{1,0:T(8,128)(2,1)S(1)}, bf16[256,512]{1,0:T(8,128)(2,1)S(1)}, u32[]{:S(2)}, u32[]{:S(2)}) collective-permute-start(bf16[256,512]{1,0:T(8,128)(2,1)S(1)} %add_convert_fusion), channel_id=1, source_target_pairs={{0,256},{128,384},{256,0},{384,128},{1,257},{129,385},{257,1},{385... | collective-permute-start | bytes 786440 | tf_op jit(solution)/shard_map/ppermute | solution.py:253
  87.1 5.3 %collective-permute-start.3 = (bf16[256,512]{1,0:T(8,128)(2,1)S(1)}, bf16[256,512]{1,0:T(8,128)(2,1)S(1)}, u32[]{:S(2)}, u32[]{:S(2)}) collective-permute-start(bf16[256,512]{1,0:T(8,128)(2,1)S(1)} %get-tuple-element.25), channel_id=1, source_target_pairs={{0,128},{128,0},{256,384},{384,256},{1,129},{129,1},{257,385},{385... | collective-permute-start | bytes 786440 | tf_op jit(solution)/shard_map/ppermute | solution.py:253
  125.3 3.8 %collective-permute-start.4 = (bf16[2,256,512]{2,1,0:T(8,128)(2,1)S(1)}, bf16[2,256,512]{2,1,0:T(8,128)(2,1)S(1)}, u32[]{:S(2)}, u32[]{:S(2)}) collective-permute-start(bf16[2,256,512]{2,1,0:T(8,128)(2,1)S(1)} %shard_map.45), channel_id=1, source_target_pairs={{0,128},{128,0},{256,384},{384,256},{1,129},{129,1},{257,385},{385... | collective-permute-start | bytes 1572872 | tf_op jit(solution)/shard_map/ppermute | solution.py:253

commit v4 on v1

--- a/solution.py
+++ b/solution.py
@@ -18,7 +18,7 @@
     return [
         [row * RING * RING + place for place in group]
         for row in range(rows)
-        for group in (first if row % 2 == 0 else second)
+        for group in (first if row in (0, 3) else second)
     ]
 
 
@@ -127,7 +127,7 @@
         lefts = []
         for q in held:
             place = (where[1] + step_along_x(where[1] ^ q)) & (RING - 1)
-            place = jnp.where((where[1] & 1) == 0, a * RING + place, place * RING + a)
+            place = jnp.where(((where[1] ^ (where[1] // 2)) & 1) == 0, a * RING + place, place * RING + a)
             at = pl.multiple_of(place * rows, rows)
             lefts.append(left[pl.ds(at, rows), :])
         if len(right.shape) == 2:

time: 154 us -> 150 us (0.974)
  the two profiles are of different devices: /device:TPU:8 before, /device:TPU:6 now
where the time goes in v4:
time: 150 us; the launch traced here: 148 us
  blocking collectives  109 us (73%)
  Pallas kernels  13.6 us (9%)
  starting transfers between devices  11.6 us (8%)
  waiting for transfers between devices  7.98 us (5%)
  local copies, waits for them, and re-layouts  3.22 us (2%)
  other arithmetic  2.53 us (2%)
    all_gather x2, blocking collectives, gather_col(): lax.all_gather(value, ('row', 'col'), axis=0, tiled=True, axis_index_grou...  56.8 us
    all_gather x1, blocking collectives, shards(): squares = lax.all_gather(square, 'depth', axis=0).astype(BF16)  31.2 us
    all_to_all x1, blocking collectives, trade_over_chip_and_depth(): lax.all_to_all(value, ('row', 'depth'), 0, 0, tiled=True, axis_index_grou...  21.2 us
    ppermute x4, starting transfers between devices, swap_row(): return lax.ppermute(value, 'row', [(r, r ^ bit) for r in range(rows)])  7.93 us
    pallas_call x5, Pallas kernels, terms_of(): call(functools.partial(terms_kernel, held, scale), flops=2 * rows * len(h...  7.84 us
    ppermute x4, waiting for transfers between devices, swap_row(): return lax.ppermute(value, 'row', [(r, r ^ bit) for r in range(rows)])  4.81 us
    ppermute x1, starting transfers between devices, trade_x_and_row(): return lax.ppermute(value, ('row', 'col'), route)  3.72 us
    unnamed x8, local copies, waits for them, and re-layouts  3.19 us
  transfers between devices with their start and end apart: 5, of which 4 were waited for; matrix products, arithmetic and copies ran while one was open for 0% of the time, Pallas kernels for 5%

profile of v4, /device:TPU:6, one launch (start us, length us, event | category | flops | bytes accessed | tf_op | source)
XLA Modules:
  0.0 148.4 jit_solution(2643757794900354465)
XLA Ops:
  0.0 1.9 %shard_map.40 = bf16[256,512]{1,0:T(8,128)(2,1)} custom-call(s32[1]{0:T(128)} %bitcast.1.where, s32[8,32]{1,0:T(8,128)} %bitcast.18, bf16[4,8,64,512]{3,2,1,0:T(8,128)(2,1)} %bitcast.13), custom_call_target="tpu_custom_call" | custom-call | bytes 1048576 | tf_op jit(solution)/shard_map/pallas_call | solution.py:61
  1.9 1.0 convert_element_type.36
  2.9 3.7 %collective-permute-start = (f16[256,512]{1,0:T(8,128)(2,1)S(1)}, f16[256,512]{1,0:T(8,128)(2,1)S(1)}, u32[]{:S(2)}, u32[]{:S(2)}) collective-permute-start(f16[256,512]{1,0:T(8,128)(2,1)S(1)} %convert_element_type.36), channel_id=1, source_target_pairs={{0,0},{8,8},{16,16},{24,24},{32,160},{40,168},{48,176},{56,184},{6... | collective-permute-start | bytes 786440 | tf_op jit(solution)/shard_map/ppermute | solution.py:258
  6.7 1.6 %copy-done = bf16[2048,512]{1,0:T(8,128)(2,1)S(1)} copy-done((bf16[2048,512]{1,0:T(8,128)(2,1)S(1)}, bf16[2048,512]{1,0:T(8,128)(2,1)}, u32[]{:S(2)}) %copy-start) | copy-done | bytes 2097176
  8.9 1.6 %copy-done.1 = bf16[2048,512]{1,0:T(8,128)(2,1)S(1)} copy-done((bf16[2048,512]{1,0:T(8,128)(2,1)S(1)}, bf16[2048,512]{1,0:T(8,128)(2,1)}, u32[]{:S(2)}) %copy-start.1) | copy-done | bytes 2097176
  10.5 0.8 shard_map.39.own
  11.3 0.9 shard_map.38
  12.2 3.2 %collective-permute-done = f16[256,512]{1,0:T(8,128)(2,1)S(1)} collective-permute-done((f16[256,512]{1,0:T(8,128)(2,1)S(1)}, f16[256,512]{1,0:T(8,128)(2,1)S(1)}, u32[]{:S(2)}, u32[]{:S(2)}) %collective-permute-start) | collective-permute-done | bytes 262176 | tf_op jit(solution)/shard_map/ppermute | solution.py:258
  15.4 13.8 %all-gather.4 = f16[1024,512]{1,0:T(8,128)(2,1)S(1)} all-gather(f16[256,512]{1,0:T(8,128)(2,1)S(1)} %collective-permute-done), channel_id=1, replica_groups={{0,32,64,96},{8,40,72,104},{16,48,80,112},{24,56,88,120},{128,136,144,1..., dimensions={0}, use_global_device_ids=true | all-gather | bytes 1310720 | tf_op jit(solution)/shard_map/all_gather | solution.py:245
  29.2 43.0 %all-gather.5 = f16[4096,512]{1,0:T(8,128)(2,1)S(1)} all-gather(f16[1024,512]{1,0:T(8,128)(2,1)S(1)} %all-gather.4), channel_id=1, replica_groups={{0,8,16,24},{32,40,48,56},{64,72,80,88},{96,104,112,120},{128,160,192,2..., dimensions={0}, use_global_device_ids=true | all-gather | bytes 5242880 | tf_op jit(solution)/shard_map/all_gather | solution.py:245
  72.2 0.8 convert_element_type.37.left
  73.0 1.2 shard_map.42
  74.2 1.9 %collective-permute-start.1 = (bf16[256,512]{1,0:T(8,128)(2,1)S(1)}, bf16[256,512]{1,0:T(8,128)(2,1)S(1)}, u32[]{:S(2)}, u32[]{:S(2)}) collective-permute-start(bf16[256,512]{1,0:T(8,128)(2,1)S(1)} %shard_map.42), channel_id=1, source_target_pairs={{0,128},{128,0},{256,384},{384,256},{1,129},{129,1},{257,385},{385... | collective-permute-start | bytes 786440 | tf_op jit(solution)/shard_map/ppermute | solution.py:250
  76.2 1.2 shard_map.41
  77.7 1.9 %collective-permute-start.2 = (bf16[256,512]{1,0:T(8,128)(2,1)S(1)}, bf16[256,512]{1,0:T(8,128)(2,1)S(1)}, u32[]{:S(2)}, u32[]{:S(2)}) collective-permute-start(bf16[256,512]{1,0:T(8,128)(2,1)S(1)} %add_convert_fusion), channel_id=1, source_target_pairs={{0,256},{128,384},{256,0},{384,128},{1,257},{129,385},{257,1},{385... | collective-permute-start | bytes 786440 | tf_op jit(solution)/shard_map/ppermute | solution.py:250
  79.7 1.8 %shard_map.43 = (bf16[256,512]{1,0:T(8,128)(2,1)S(1)}, bf16[256,512]{1,0:T(8,128)(2,1)S(1)}) custom-call(s32[3]{0:T(128)S(1)} %pad_add_fusion.where, bf16[2048,512]{1,0:T(8,128)(2,1)S(1)} %shard_map.37.right, bf16[4096,512]{1,0:T(8,128)(2,1)S(1)} %convert_element_type.37.left), custom_call_target="tpu_custom_call" | custom-call | flops 1073741824 | bytes 4718592 | tf_op jit(solution)/shard_map/pallas_call | solution.py:155
  81.5 2.2 %collective-permute-start.3 = (bf16[256,512]{1,0:T(8,128)(2,1)S(1)}, bf16[256,512]{1,0:T(8,128)(2,1)S(1)}, u32[]{:S(2)}, u32[]{:S(2)}) collective-permute-start(bf16[256,512]{1,0:T(8,128)(2,1)S(1)} %get-tuple-element.25), channel_id=1, source_target_pairs={{0,128},{128,0},{256,384},{384,256},{1,129},{129,1},{257,385},{385... | collective-permute-start | bytes 786440 | tf_op jit(solution)/shard_map/ppermute | solution.py:250
  83.6 4.5 %collective-permute-done.2 = bf16[256,512]{1,0:T(8,128)(2,1)S(1)} collective-permute-done((bf16[256,512]{1,0:T(8,128)(2,1)S(1)}, bf16[256,512]{1,0:T(8,128)(2,1)S(1)}, u32[]{:S(2)}, u32[]{:S(2)}) %collective-permute-start.2) | collective-permute-done | bytes 262176 | tf_op jit(solution)/shard_map/ppermute | solution.py:250
  88.3 31.2 %all-gather.6 = f16[2048,512]{1,0:T(8,128)(2,1)S(1)} all-gather(f16[256,512]{1,0:T(8,128)(2,1)S(1)} %fusion), channel_id=2, replica_groups=mesh['row'=4,'col'=16,'depth'=8] {'depth'}, dimensions={0}, use_global_device_ids=true | all-gather | bytes 2359296 | tf_op jit(solution)/shard_map/all_gather | solution.py:297
  119.9 1.8 %shard_map.45 = bf16[2,256,512]{2,1,0:T(8,128)(2,1)S(1)} custom-call(s32[3]{0:T(128)S(1)} %pad_add_fusion.where, bf16[8,256,512]{2,1,0:T(8,128)(2,1)S(1)} %bitcast.15, bf16[4096,512]{1,0:T(8,128)(2,1)S(1)} %convert_element_type.37.left), custom_call_target="tpu_custom_call" | custom-call | flops 1073741824 | bytes 4718592 | tf_op jit(solution)/shard_map/pallas_call | solution.py:155
  121.7 1.9 %collective-permute-start.4 = (bf16[2,256,512]{2,1,0:T(8,128)(2,1)S(1)}, bf16[2,256,512]{2,1,0:T(8,128)(2,1)S(1)}, u32[]{:S(2)}, u32[]{:S(2)}) collective-permute-start(bf16[2,256,512]{2,1,0:T(8,128)(2,1)S(1)} %shard_map.45), channel_id=1, source_target_pairs={{0,128},{128,0},{256,384},{384,256},{1,129},{129,1},{257,385},{385... | collective-permute-start | bytes 1572872 | tf_op jit(solution)/shard_map/ppermute | solution.py:250
  123.6 1.8 %shard_map.44 = (bf16[256,512]{1,0:T(8,128)(2,1)S(1)}, bf16[256,512]{1,0:T(8,128)(2,1)S(1)}) custom-call(s32[3]{0:T(128)S(1)} %pad_add_fusion.where, bf16[8,256,512]{2,1,0:T(8,128)(2,1)S(1)} %bitcast.16, bf16[4096,512]{1,0:T(8,128)(2,1)S(1)} %convert_element_type.37.left), custom_call_target="tpu_custom_call" | custom-call | flops 1073741824 | bytes 4718592 | tf_op jit(solution)/shard_map/pallas_call | solution.py:155
  126.3 21.2 %all_to_all.5.got = bf16[16,64,256]{2,1,0:T(8,128)(2,1)S(1)} all-to-all(bf16[16,64,256]{2,1,0:T(8,128)(2,1)S(1)} %bitcast.17), channel_id=1, replica_groups={{0,1,2,3,4,5,6,7,256,257,258,259,260,261,262,263},{128,129,130,131,132,..., dimensions={0} | all-to-all | bytes 1048576 | tf_op jit(solution)/shard_map/all_to_all | solution.py:281
  147.5 0.9 shard_map.47
  (16 shorter events, 2.4 us)
Async XLA Ops:
  0.0 6.6 %copy-start.3 = (s32[32,8]{0,1:T(8,128)S(1)}, s32[32,8]{0,1:T(8,128)}, u32[]{:S(2)}) copy-start(s32[32,8]{0,1:T(8,128)} %param.4) | copy-start | bytes 3076
  2.9 12.4 %collective-permute-start = (f16[256,512]{1,0:T(8,128)(2,1)S(1)}, f16[256,512]{1,0:T(8,128)(2,1)S(1)}, u32[]{:S(2)}, u32[]{:S(2)}) collective-permute-start(f16[256,512]{1,0:T(8,128)(2,1)S(1)} %convert_element_type.36), channel_id=1, source_target_pairs={{0,0},{8,8},{16,16},{24,24},{32,160},{40,168},{48,176},{56,184},{6... | collective-permute-start | bytes 786440 | tf_op jit(solution)/shard_map/ppermute | solution.py:258
  6.7 1.6 %copy-start = (bf16[2048,512]{1,0:T(8,128)(2,1)S(1)}, bf16[2048,512]{1,0:T(8,128)(2,1)}, u32[]{:S(2)}) copy-start(bf16[2048,512]{1,0:T(8,128)(2,1)} %rows.1) | copy-start | bytes 6291460
  8.2 3.1 %copy-start.2 = (s32[128,128]{1,0:T(8,128)S(1)}, s32[128,128]{1,0:T(8,128)}, u32[]{:S(2)}) copy-start(s32[128,128]{1,0:T(8,128)} %filtering.1) | copy-start | bytes 196612
  8.9 1.6 %copy-start.1 = (bf16[2048,512]{1,0:T(8,128)(2,1)S(1)}, bf16[2048,512]{1,0:T(8,128)(2,1)}, u32[]{:S(2)}) copy-start(bf16[2048,512]{1,0:T(8,128)(2,1)} %rows.1) | copy-start | bytes 6291460
  74.2 3.4 %collective-permute-start.1 = (bf16[256,512]{1,0:T(8,128)(2,1)S(1)}, bf16[256,512]{1,0:T(8,128)(2,1)S(1)}, u32[]{:S(2)}, u32[]{:S(2)}) collective-permute-start(bf16[256,512]{1,0:T(8,128)(2,1)S(1)} %shard_map.42), channel_id=1, source_target_pairs={{0,128},{128,0},{256,384},{384,256},{1,129},{129,1},{257,385},{385... | collective-permute-start | bytes 786440 | tf_op jit(solution)/shard_map/ppermute | solution.py:250
  77.7 10.4 %collective-permute-start.2 = (bf16[256,512]{1,0:T(8,128)(2,1)S(1)}, bf16[256,512]{1,0:T(8,128)(2,1)S(1)}, u32[]{:S(2)}, u32[]{:S(2)}) collective-permute-start(bf16[256,512]{1,0:T(8,128)(2,1)S(1)} %add_convert_fusion), channel_id=1, source_target_pairs={{0,256},{128,384},{256,0},{384,128},{1,257},{129,385},{257,1},{385... | collective-permute-start | bytes 786440 | tf_op jit(solution)/shard_map/ppermute | solution.py:250
  81.5 6.6 %collective-permute-start.3 = (bf16[256,512]{1,0:T(8,128)(2,1)S(1)}, bf16[256,512]{1,0:T(8,128)(2,1)S(1)}, u32[]{:S(2)}, u32[]{:S(2)}) collective-permute-start(bf16[256,512]{1,0:T(8,128)(2,1)S(1)} %get-tuple-element.25), channel_id=1, source_target_pairs={{0,128},{128,0},{256,384},{384,256},{1,129},{129,1},{257,385},{385... | collective-permute-start | bytes 786440 | tf_op jit(solution)/shard_map/ppermute | solution.py:250
  121.7 3.8 %collective-permute-start.4 = (bf16[2,256,512]{2,1,0:T(8,128)(2,1)S(1)}, bf16[2,256,512]{2,1,0:T(8,128)(2,1)S(1)}, u32[]{:S(2)}, u32[]{:S(2)}) collective-permute-start(bf16[2,256,512]{2,1,0:T(8,128)(2,1)S(1)} %shard_map.45), channel_id=1, source_target_pairs={{0,128},{128,0},{256,384},{384,256},{1,129},{129,1},{257,385},{385... | collective-permute-start | bytes 1572872 | tf_op jit(solution)/shard_map/ppermute | solution.py:250
